TPU v7x, 256 devices: a whole 4x4x8 slice. The times are simulated.
256 devices in a mesh: wall: 32 (over y, z), span: 2 (over x_hi), stream: 4 (over x_lo, core).
Axes of the slice: x: 4 (x_hi: 2, x_lo: 2; x = x_hi * 2 + x_lo), y: 4, z: 8, core: 2. Of those that a mesh axis runs over, the one named last changes fastest.
Arguments:
- right_side: float32 [1024, 128, 512], P('wall', 'span', 'stream'), may hold values from -6 to 6
- viscosity: float32 [1024, 128, 512], P('wall', 'span', 'stream'), may hold values from 0.05 to 1
- wall_metric: float32 [1024], P('wall'), may hold values from 0.5 to 4
- line_inverse: bfloat16 [1024, 1024], replicated
Outputs:
- solution: float32 [1024, 128, 512], P('wall', 'span', 'stream')
- residual: float32 [1024, 128, 512], P('wall', 'span', 'stream')
All inputs are finite; a program needn't handle non-finite values.
Results may differ from a plain program's by a relative error of at most 0.0057.
Values may be sent and summed in bfloat16 or wider, within the bound.
No kernel may reach another device: no remote copies, remote signals or barrier semaphores. Data moves between devices by JAX's collectives and lax.ppermute only.
A program may use at most 128 MiB of HBM per device.

v0:
```python
import functools

import jax
import jax.numpy as jnp
from jax import lax
from jax.experimental import pallas as pl
from jax.experimental.pallas import tpu as pltpu
from jax.sharding import PartitionSpec as P

STEPS = 3
NW, WY, WZ = 1024, 4, 8
ROWS, SPAN, LANES = 32, 64, 128
BS, BX = 16, 16
CELLS = BS * BX
TAIL = 8
MID = 0.5
F32, BF16 = jnp.float32, jnp.bfloat16
VMEM = pl.BlockSpec(memory_space=pltpu.VMEM)
PARAMS = pltpu.CompilerParams(vmem_limit_bytes=40 * 1024 * 1024)


def chebyshev_weights(steps):
    lowest = 0.25
    highest = 2.5
    center = 0.5 * (highest + lowest)
    half = 0.5 * (highest - lowest)
    ratio = center / half
    weights = [(0.0, 1.0 / center)]
    rho_old = 1.0 / ratio
    for step in range(1, steps):
        rho_new = 1.0 / (2.0 * ratio - rho_old)
        weights.append((rho_new * rho_old, 2.0 * rho_new / half))
        rho_old = rho_new
    return weights


WEIGHTS = chebyshev_weights(STEPS)


def shape(dims, dtype):
    return jax.ShapeDtypeStruct(dims, dtype)


def call(kernel, outs, scratch=(), **cost):
    return pl.pallas_call(
        kernel,
        out_shape=outs,
        scratch_shapes=list(scratch),
        compiler_params=PARAMS,
        cost_estimate=pl.CostEstimate(
            flops=cost.get("flops", 10**7), bytes_accessed=cost.get("size", 4 * 10**6), transcendentals=0
        ),
    )


def lane_blocks(rows):
    block = lax.broadcasted_iota(jnp.int32, rows[0].shape, 1) // BX
    rows = list(rows)
    for bit in range(3):
        step = 1 << bit
        upper = (block // step) % 2 == 1
        for i in range(8):
            if i & step:
                continue
            a, b = rows[i], rows[i + step]
            rows[i] = jnp.where(upper, pltpu.roll(b, BX * step, 1), a)
            rows[i + step] = jnp.where(upper, b, pltpu.roll(a, LANES - BX * step, 1))
    return rows


def strided(s):
    return pl.ds(s, ROWS, stride=SPAN)


def pack(b_ref, v_ref, m_ref, send, ew0, ew1, es, exl, exr):
    m = m_ref[...]
    rest = m
    parts = []
    for _ in range(3):
        part = rest.astype(BF16)
        rest = rest - part.astype(F32)
        parts.append(part.astype(F32))
    tail = jnp.concatenate(parts + [jnp.zeros((TAIL - 3, ROWS), F32)], axis=0)
    tail = jnp.concatenate([tail, jnp.zeros((TAIL, LANES - ROWS), F32)], axis=1).astype(BF16)
    for k in range(WY * WZ):
        send[k, 4 * ROWS :, :] = tail
    for t in range(WY):
        for g in range(2):
            for ref, off, mid in ((b_ref, 0, 0.0), (v_ref, 2, MID)):
                parts = lane_blocks([ref[strided(16 * t + 8 * g + i), :] - mid for i in range(8)])
                rows = slice(ROWS * (off + g), ROWS * (off + g + 1))
                for z in range(WZ):
                    send[WZ * t + z, rows, :] = parts[z].astype(BF16)
                if off:
                    exl[2 * t + g] = parts[0].astype(BF16)
                    exr[2 * t + g] = parts[7].astype(BF16)
    ew0[...] = v_ref[0:SPAN, :] * m[:, :1]
    ew1[...] = v_ref[(ROWS - 1) * SPAN :, :] * m[:, ROWS - 1 :]
    es[0] = (v_ref[strided(0), :] - MID).astype(BF16)
    es[1] = (v_ref[strided(SPAN - 1), :] - MID).astype(BF16)


def to_lines(recv, bt, vt, metric, *edges):
    for i in range(8):
        row = jnp.zeros((TAIL, LANES), F32)
        for j in range(4):
            row += pltpu.roll(recv[4 * i + j, 4 * ROWS :, :].astype(F32), ROWS * j, 1)
        metric[:, i * LANES : (i + 1) * LANES] = jnp.sum(row, axis=0, keepdims=True)
    for j in range(4):
        for i in range(8):
            tile = recv[4 * i : 4 * i + 4, ROWS * j : ROWS * (j + 1), :].astype(F32).reshape(LANES, LANES).T
            out = bt if j < 2 else vt
            out[(j % 2) * LANES : (j % 2 + 1) * LANES, i * LANES : (i + 1) * LANES] = tile.astype(BF16)
    for k, ref in enumerate((bt, vt)):
        grid = ref[...].astype(F32).reshape(BS, BX, NW)
        rows = slice(BX * k, BX * (k + 1))
        edges[0][rows] = grid[0].astype(BF16)
        edges[1][rows] = grid[BS - 1].astype(BF16)
        edges[2][rows] = grid[:, 0, :].astype(BF16)
        edges[3][rows] = grid[:, BX - 1, :].astype(BF16)


def apply_lines(rows, line):
    return lax.dot_general(rows, line, (((1,), (1,)), ((), ())), preferred_element_type=F32)


def first_lines(bt, line, x1):
    x1[...] = WEIGHTS[0][1] * apply_lines(bt[...], line[...])


def fill(ext, middle, su, sd, xl, xr):
    ext[1 : BS + 1, 8 : 8 + BX, :] = middle
    ext[0, 8 : 8 + BX, :] = su
    ext[BS + 1, 8 : 8 + BX, :] = sd
    for s in range(BS):
        ext[s + 1, 7:8, :] = xl[s : s + 1]
        ext[s + 1, 8 + BX : 9 + BX, :] = xr[s : s + 1]


def line_resid(s, bt, xe, ve, metric, out):
    lane = lax.broadcasted_iota(jnp.int32, (BX, LANES), 1)
    count = NW // LANES

    def load(ref, j):
        lanes = slice(j * LANES, (j + 1) * LANES)
        return ref[s + 1, 8 : 8 + BX, lanes]

    xs = [load(xe, j) for j in range(count)]
    ks = [load(ve, j) * metric[:, j * LANES : (j + 1) * LANES] for j in range(count)]
    zero = jnp.zeros((BX, LANES), F32)
    xroll = [pltpu.roll(v, LANES - 1, 1) for v in xs] + [zero]
    kroll = [pltpu.roll(v, LANES - 1, 1) for v in ks] + [zero]
    last = lane == LANES - 1
    first = lane == 0
    carry = None
    for j in range(count):
        lanes = slice(j * LANES, (j + 1) * LANES)
        xc, kc = xs[j], ks[j]
        xn = jnp.where(last, xroll[j + 1], xroll[j])
        kn = jnp.where(last, kroll[j + 1], kroll[j])
        above = (kc + kn) * (xc - xn)
        moved = pltpu.roll(above, 1, 1)
        entry = kc * xc if j == 0 else carry
        total = above - jnp.where(first, entry if j else -entry, moved)
        carry = moved
        vc = ve[s + 1, 8 : 8 + BX, lanes]
        for si, x0 in ((s, 8), (s + 2, 8), (s + 1, 7), (s + 1, 9)):
            total += (vc + ve[si, x0 : x0 + BX, lanes]) * (xc - xe[si, x0 : x0 + BX, lanes])
        resid = bt[pl.ds(pl.multiple_of(s * BX, BX), BX), lanes].astype(F32) - (xc + 0.5 * total)
        out[pl.ds(pl.multiple_of(s * BX, BX), BX), lanes] = resid.astype(BF16)


def second_step(
    x1, bt, vt, su, sd, xl, xr, line, metric, x2, d2, e0, e1, e2, e3, xe, ve, rt, ends
):
    for k, ref in enumerate((su, sd, xl, xr)):
        ends[k * BX : (k + 1) * BX] = ref[0:BX]
    ends1 = WEIGHTS[0][1] * apply_lines(ends[...], line[...])
    fill(xe, x1[...].reshape(BS, BX, NW), *(ends1[k * BX : (k + 1) * BX] for k in range(4)))
    fill(
        ve,
        vt[...].astype(F32).reshape(BS, BX, NW) + MID,
        *(ref[BX : 2 * BX].astype(F32) + MID for ref in (su, sd, xl, xr)),
    )

    def one(s, _):
        line_resid(s, bt, xe, ve, metric, rt)
        return 0

    lax.fori_loop(0, BS, one, 0)
    keep, scale = WEIGHTS[1]
    d2[...] = keep * x1[...] + scale * apply_lines(rt[...], line[...])
    x2[...] = x1[...] + d2[...]
    grid = x2[...].reshape(BS, BX, NW)
    e0[...] = grid[0]
    e1[...] = grid[BS - 1]
    e2[...] = grid[:, 0, :]
    e3[...] = grid[:, BX - 1, :]


def third_step(x2, d2, bt, vt, su, sd, xl, xr, vsu, vsd, vxl, vxr, line, metric, send, xe, ve, rt, x3):
    fill(xe, x2[...].reshape(BS, BX, NW), su[...], sd[...], xl[...], xr[...])
    fill(
        ve,
        vt[...].astype(F32).reshape(BS, BX, NW) + MID,
        *(ref[BX : 2 * BX].astype(F32) + MID for ref in (vsu, vsd, vxl, vxr)),
    )

    def one(s, _):
        line_resid(s, bt, xe, ve, metric, rt)
        return 0

    lax.fori_loop(0, BS, one, 0)
    keep, scale = WEIGHTS[2]
    x3[...] = x2[...] + keep * d2[...] + scale * apply_lines(rt[...], line[...])
    for j in range(2):
        for i in range(8):
            tile = x3[j * LANES : (j + 1) * LANES, i * LANES : (i + 1) * LANES].T
            send[i * LANES : (i + 1) * LANES, j * LANES : (j + 1) * LANES] = tile.astype(BF16)


def unpack(recv, x3, xs, ew0, ew1, es, exl, exr):
    for t in range(WY):
        for g in range(2):
            lanes = slice(LANES * g, LANES * (g + 1))
            parts = [recv[WZ * t + z, :, lanes] for z in range(WZ)]
            exl[2 * t + g] = parts[0]
            exr[2 * t + g] = parts[7]
            parts = lane_blocks([p.astype(F32) for p in parts])
            for i in range(8):
                s = 16 * t + 8 * g + i
                x3[strided(s), :] = parts[i]
                xs[s] = parts[i]
    ew0[...] = x3[0:SPAN, :]
    ew1[...] = x3[(ROWS - 1) * SPAN :, :]
    es[0] = xs[0].astype(BF16)
    es[1] = xs[SPAN - 1].astype(BF16)


def last_resid(
    xs, v_ref, b_ref, m_ref, xdn, xup, xsp, xlf, xrt, kdn, kup, vsp, vlf, vrt, out, xe, ve
):
    xe[1 : SPAN + 1] = xs[...]
    xe[0] = xsp[1].astype(F32)
    xe[SPAN + 1] = xsp[0].astype(F32)
    for s in range(SPAN):
        ve[s + 1] = v_ref[strided(s), :]
    ve[0] = vsp[1].astype(F32) + MID
    ve[SPAN + 1] = vsp[0].astype(F32) + MID
    row = lax.broadcasted_iota(jnp.int32, (ROWS, LANES), 0)
    lane = lax.broadcasted_iota(jnp.int32, (ROWS, LANES), 1)
    square = lax.broadcasted_iota(jnp.int32, (ROWS, ROWS), 0)
    square = square == lax.broadcasted_iota(jnp.int32, (ROWS, ROWS), 1)
    m = jnp.sum(jnp.where(square, m_ref[...], 0.0), axis=1, keepdims=True)

    def eight(q, _):
        rows = pl.ds(pl.multiple_of(8 * q, 8), 8)
        beyond = [ref[rows, :] for ref in (xdn, xup, kdn, kup)]
        for i in range(8):
            s = 8 * q + i
            xc, vc = xe[s + 1], ve[s + 1]
            total = (vc + ve[s]) * (xc - xe[s]) + (vc + ve[s + 2]) * (xc - xe[s + 2])
            xb, xa, kb, ka = (block[i : i + 1] for block in beyond)
            xn = jnp.where(row == 0, xb, pltpu.roll(xc, 1, 0))
            kc = m * vc
            kn = jnp.where(row == 0, kb, pltpu.roll(kc, 1, 0))
            total += (kc + kn) * (xc - xn)
            xn = jnp.where(row == ROWS - 1, xa, pltpu.roll(xc, ROWS - 1, 0))
            kn = jnp.where(row == ROWS - 1, ka, pltpu.roll(kc, ROWS - 1, 0))
            total += (kc + kn) * (xc - xn)
            left = (LANES - (BX * i + BX - 1)) % LANES
            xn = jnp.where(lane == 0, pltpu.roll(xlf[q].astype(F32), left, 1), pltpu.roll(xc, 1, 1))
            vn = jnp.where(
                lane == 0, pltpu.roll(vlf[q].astype(F32) + MID, left, 1), pltpu.roll(vc, 1, 1)
            )
            total += (vc + vn) * (xc - xn)
            right = LANES - 1 - BX * i
            xn = jnp.where(
                lane == LANES - 1,
                pltpu.roll(xrt[q].astype(F32), right, 1),
                pltpu.roll(xc, LANES - 1, 1),
            )
            vn = jnp.where(
                lane == LANES - 1,
                pltpu.roll(vrt[q].astype(F32) + MID, right, 1),
                pltpu.roll(vc, LANES - 1, 1),
            )
            total += (vc + vn) * (xc - xn)
            out[strided(s), :] = b_ref[strided(s), :] - (xc + 0.5 * total)
        return 0

    lax.fori_loop(0, SPAN // 8, eight, 0)


def block_edges(ew0, ew1, es, exl, exr):
    walls = lax.axis_size("wall")
    streams = lax.axis_size("stream")
    rising = [(i, i + 1) for i in range(walls - 1)]
    falling = [(i + 1, i) for i in range(walls - 1)]
    right = [(i, (i + 1) % streams) for i in range(streams)]
    left = [((i + 1) % streams, i) for i in range(streams)]
    return (
        lax.ppermute(ew1, "wall", rising),
        lax.ppermute(ew0, "wall", falling),
        lax.ppermute(es, "span", [(0, 1), (1, 0)]),
        lax.ppermute(exr, "stream", right),
        lax.ppermute(exl, "stream", left),
    )


def line_shift(value, ds, dx):
    spans, streams = lax.axis_size("span"), lax.axis_size("stream")
    pairs = []
    for y in range(WY):
        for z in range(WZ):
            for sp in range(spans):
                for st in range(streams):
                    sb = (sp * WY + y + ds) % (spans * WY)
                    xb = (st * WZ + z + dx) % (streams * WZ)
                    here = ((y * WZ + z) * spans + sp) * streams + st
                    there = ((sb % WY) * WZ + xb % WZ) * spans + sb // WY
                    pairs.append((here, there * streams + xb // WZ))
    return lax.ppermute(value, ("wall", "span", "stream"), pairs)


def line_edges(*edges):
    return (
        line_shift(edges[1], 1, 0),
        line_shift(edges[0], -1, 0),
        line_shift(edges[3], 0, 1),
        line_shift(edges[2], 0, -1),
    )


def body(right_side, viscosity, wall_metric, line_inverse):
    b = right_side.reshape(ROWS * SPAN, LANES)
    v = viscosity.reshape(ROWS * SPAN, LANES)
    m = wall_metric.reshape(1, ROWS)
    chunk = shape((2 * WY, ROWS, LANES), BF16)
    wide = shape((SPAN, LANES), F32)
    deep = shape((2, ROWS, LANES), BF16)
    block_outs = (wide, wide, deep, chunk, chunk)
    send, *edges = call(pack, (shape((WY * WZ, 4 * ROWS + TAIL, LANES), BF16), *block_outs))(b, v, m)
    v_edges = block_edges(*edges)
    recv = lax.all_to_all(send, "wall", 0, 0, tiled=True)
    lines = shape((CELLS, NW), BF16)
    bt, vt, metric, *edges = call(
        to_lines, (lines, lines, shape((1, NW), F32)) + (shape((2 * BX, NW), BF16),) * 4
    )(recv)
    near = line_edges(*edges)
    x1 = call(first_lines, shape((CELLS, NW), F32))(bt, line_inverse)
    ext = pltpu.VMEM((BS + 2, 2 * BX, NW), F32)
    field = shape((CELLS, NW), F32)
    rounded = pltpu.VMEM((CELLS, NW), BF16)
    x2, d2, *edges = call(
        second_step,
        (field, field) + (shape((BX, NW), F32),) * 4,
        (ext, ext, rounded, pltpu.VMEM((4 * BX, NW), BF16)),
    )(x1, bt, vt, *near, line_inverse, metric)
    x_near = line_edges(*edges)
    send = call(
        third_step,
        shape((NW, CELLS), BF16),
        (ext, ext, rounded, pltpu.VMEM((CELLS, NW), F32)),
    )(x2, d2, bt, vt, *x_near, *near, line_inverse, metric)
    recv = lax.all_to_all(send.reshape(WY * WZ, ROWS, CELLS), "wall", 0, 0, tiled=True)
    x3, xs, *edges = call(
        unpack,
        (shape((ROWS * SPAN, LANES), F32), shape((SPAN, ROWS, LANES), F32), *block_outs),
    )(recv)
    x_edges = block_edges(*edges)
    tall = pltpu.VMEM((SPAN + 2, ROWS, LANES), F32)
    residual = call(last_resid, shape((ROWS * SPAN, LANES), F32), (tall, tall))(
        xs, v, b, m, *x_edges, *v_edges
    )
    dims = right_side.shape
    return x3.reshape(dims), residual.reshape(dims)


def solution(mesh):
    in_specs = (P("wall", "span", "stream"), P("wall", "span", "stream"), P("wall"), P())
    out_specs = (P("wall", "span", "stream"), P("wall", "span", "stream"))
    return jax.shard_map(body, mesh=mesh, in_specs=in_specs, out_specs=out_specs, check_vma=False)
```

profile of v0, /device:TPU:1, one launch (start us, length us, event | category | flops | bytes accessed | tf_op | source)
XLA Modules:
  0.0 125.5 jit_solution(11239941242616338831)
XLA Ops:
  0.6 1.2 copy-done.1
  1.9 1.2 copy-done.3
  3.7 2.9 %shard_map.59 = (bf16[32,136,128]{2,1,0:T(8,128)(2,1)S(1)}, f32[64,128]{1,0:T(8,128)S(1)}, f32[64,128]{1,0:T(8,128)S(1)}, bf16[2,32,128]{2,1,0:T(8,128)(2,1)S(1)...) custom-call(f32[2048,128]{1,0:T(8,128)S(1)} %bitcast.6, f32[2048,128]{1,0:T(8,128)S(1)} %bitcast.8, ...), custom_call_target="tpu_custom_call" | custom-call | flops 10000000 | bytes 4000000 | tf_op jit(solution)/shard_map/pallas_call | solution.py:343
  6.6 42.4 %all_to_all.10.recv = bf16[32,136,128]{2,1,0:T(8,128)(2,1)S(1)} all-to-all(bf16[32,136,128]{2,1,0:T(8,128)(2,1)S(1)} %get-tuple-element.28), channel_id=1, replica_groups=mesh['wall'=32,'span'=2,'stream'=4] {'wall'}, dimensions={0} | all-to-all | bytes 2228224 | tf_op jit(solution)/shard_map/all_to_all | solution.py:345
  50.1 4.8 %collective-permute-start.1 = (bf16[32,1024]{1,0:T(8,128)(2,1)S(1)}, bf16[32,1024]{1,0:T(8,128)(2,1)S(1)}, u32[]{:S(2)}, u32[]{:S(2)}) collective-permute-start(bf16[32,1024]{1,0:T(8,128)(2,1)S(1)} %get-tuple-element.32), channel_id=1, source_target_pairs={{0,196},{1,197},{2,198},{3,199},{4,192},{5,193},{6,194},{7,195},{8... | collective-permute-start | bytes 196616 | tf_op jit(solution)/shard_map/ppermute | solution.py:323
  55.3 2.5 %collective-permute-start.3 = (bf16[32,1024]{1,0:T(8,128)(2,1)S(1)}, bf16[32,1024]{1,0:T(8,128)(2,1)S(1)}, u32[]{:S(2)}, u32[]{:S(2)}) collective-permute-start(bf16[32,1024]{1,0:T(8,128)(2,1)S(1)} %get-tuple-element.34), channel_id=1, source_target_pairs={{0,59},{1,56},{2,57},{3,58},{4,63},{5,60},{6,61},{7,62},{8,0},{9,1... | collective-permute-start | bytes 196616 | tf_op jit(solution)/shard_map/ppermute | solution.py:323
  58.6 1.2 collective-permute-done.2.xl.vxl
  59.8 4.8 %shard_map.62 = (f32[256,1024]{1,0:T(8,128)S(1)}, f32[256,1024]{1,0:T(8,128)S(1)}, f32[16,1024]{1,0:T(8,128)S(1)}, f32[16,1024]{1,0:T(8,128)S(1)}, f32[16,1024]{1,0:T(8,128)S(1)}, /*index=5*/f32[16,1024]{1,0:T(8,128)S(1)}) custom-call(f32[256,1024]{1,0:T(8,128)S(1)} %shard_map.61.x1, bf16[256,1024]{1,0:T(8,128)(2,1)S(1)} %get-tuple-element.29.bt, ...), custom_call_target="tpu_custom_call" | custom-call | flops 10000000 | bytes 4000000 | tf_op jit(solution)/shard_map/pallas_call | solution.py:355
  64.6 5.1 %collective-permute-start.5 = (f32[16,1024]{1,0:T(8,128)S(1)}, f32[16,1024]{1,0:T(8,128)S(1)}, u32[]{:S(2)}, u32[]{:S(2)}) collective-permute-start(f32[16,1024]{1,0:T(8,128)S(1)} %get-tuple-element.39), channel_id=1, source_target_pairs={{0,196},{1,197},{2,198},{3,199},{4,192},{5,193},{6,194},{7,195},{8... | collective-permute-start | bytes 196616 | tf_op jit(solution)/shard_map/ppermute | solution.py:323
  69.7 3.5 %collective-permute-start.7 = (f32[16,1024]{1,0:T(8,128)S(1)}, f32[16,1024]{1,0:T(8,128)S(1)}, u32[]{:S(2)}, u32[]{:S(2)}) collective-permute-start(f32[16,1024]{1,0:T(8,128)S(1)} %get-tuple-element.41), channel_id=1, source_target_pairs={{0,59},{1,56},{2,57},{3,58},{4,63},{5,60},{6,61},{7,62},{8,0},{9,1... | collective-permute-start | bytes 196616 | tf_op jit(solution)/shard_map/ppermute | solution.py:323
  73.2 2.2 %collective-permute-done.6.xl = f32[16,1024]{1,0:T(8,128)S(1)} collective-permute-done((f32[16,1024]{1,0:T(8,128)S(1)}, f32[16,1024]{1,0:T(8,128)S(1)}, u32[]{:S(2)}, u32[]{:S(2)}) %collective-permute-start.6) | collective-permute-done | bytes 65568 | tf_op jit(solution)/shard_map/ppermute | solution.py:323
  75.5 4.9 %shard_map.63 = bf16[1024,256]{1,0:T(8,128)(2,1)} custom-call(f32[256,1024]{1,0:T(8,128)S(1)} %get-tuple-element.36.x2, f32[256,1024]{1,0:T(8,128)S(1)} %get-tuple-element.37.d2, bf16[256,1024]{1,0:T(8,128)(2,1)S(1)} %get-tuple-element.29.bt, bf16[256,1024]{1,0:T(8,128)(2,1)S(1)} %get-tuple-element.30.vt, f32[16,1024]{1,0:T(8,128)S(1)} %collective-permute-done.4.su, ...), custom_call_target="tpu_custom_call" | custom-call | flops 10000000 | bytes 4000000 | tf_op jit(solution)/shard_map/pallas_call | solution.py:361
  80.3 9.6 %all-to-all-start.1 = ((bf16[32,32,256]{2,1,0:T(8,128)(2,1)}), bf16[32,32,256]{2,1,0:T(8,128)(2,1)S(1)}, u32[]{:S(2)}, u32[]{:S(2)}) async-start(bf16[32,32,256]{2,1,0:T(8,128)(2,1)} %bitcast.3), calls=%async_computation.1 | async-start | bytes 1048576 | tf_op jit(solution)/shard_map/all_to_all | solution.py:366
  90.0 3.1 %collective-permute-start.13 = (f32[64,128]{1,0:T(8,128)S(1)}, f32[64,128]{1,0:T(8,128)S(1)}, u32[]{:S(2)}, u32[]{:S(2)}) collective-permute-start(f32[64,128]{1,0:T(8,128)S(1)} %get-tuple-element.49), channel_id=1, source_target_pairs={{0,8},{8,16},{16,24},{24,32},{32,40},{40,48},{48,56},{56,64},{64,7... | collective-permute-start | bytes 98312 | tf_op jit(solution)/shard_map/ppermute | solution.py:303
  93.2 0.8 collective-permute-start.17
  94.0 2.5 %collective-permute-start.15 = (bf16[2,32,128]{2,1,0:T(8,128)(2,1)S(1)}, bf16[2,32,128]{2,1,0:T(8,128)(2,1)S(1)}, u32[]{:S(2)}, u32[]{:S(2)}) collective-permute-start(bf16[2,32,128]{2,1,0:T(8,128)(2,1)S(1)} %get-tuple-element.51), channel_id=1, source_target_pairs={{0,4},{4,0},{1,5},{5,1},{2,6},{6,2},{3,7},{7,3},{8,12},{12,8},{9,1... | collective-permute-start | bytes 49160 | tf_op jit(solution)/shard_map/ppermute | solution.py:305
  96.5 1.3 %collective-permute-start.14 = (f32[64,128]{1,0:T(8,128)S(1)}, f32[64,128]{1,0:T(8,128)S(1)}, u32[]{:S(2)}, u32[]{:S(2)}) collective-permute-start(f32[64,128]{1,0:T(8,128)S(1)} %get-tuple-element.50), channel_id=1, source_target_pairs={{8,0},{16,8},{24,16},{32,24},{40,32},{48,40},{56,48},{64,56},{72,6... | collective-permute-start | bytes 98312 | tf_op jit(solution)/shard_map/ppermute | solution.py:304
  97.8 9.4 %all-to-all-done.1.recv = bf16[32,32,256]{2,1,0:T(8,128)(2,1)S(1)} async-done(((bf16[32,32,256]{2,1,0:T(8,128)(2,1)}), bf16[32,32,256]{2,1,0:T(8,128)(2,1)S(1)}, u32[]{:S(2)}, u32[]{:S(2)}) %all-to-all-start.1) | async-done | bytes 524320 | tf_op jit(solution)/shard_map/all_to_all | solution.py:366
  107.2 3.0 %shard_map.64 = (f32[2048,128]{1,0:T(8,128)}, f32[64,32,128]{2,1,0:T(8,128)S(1)}, f32[64,128]{1,0:T(8,128)S(1)}, f32[64,128]{1,0:T(8,128)S(1)}, bf16[2,32,128]{2...) custom-call(bf16[32,32,256]{2,1,0:T(8,128)(2,1)S(1)} %all-to-all-done.1.recv), custom_call_target="tpu_custom_call" | custom-call | flops 10000000 | bytes 4000000 | tf_op jit(solution)/shard_map/pallas_call | solution.py:367
  110.9 3.9 %collective-permute-start.8 = (f32[64,128]{1,0:T(8,128)S(1)}, f32[64,128]{1,0:T(8,128)S(1)}, u32[]{:S(2)}, u32[]{:S(2)}) collective-permute-start(f32[64,128]{1,0:T(8,128)S(1)} %get-tuple-element.44), channel_id=1, source_target_pairs={{0,8},{8,16},{16,24},{24,32},{32,40},{40,48},{48,56},{56,64},{64,7... | collective-permute-start | bytes 98312 | tf_op jit(solution)/shard_map/ppermute | solution.py:303
  114.8 1.3 %collective-permute-start.9 = (f32[64,128]{1,0:T(8,128)S(1)}, f32[64,128]{1,0:T(8,128)S(1)}, u32[]{:S(2)}, u32[]{:S(2)}) collective-permute-start(f32[64,128]{1,0:T(8,128)S(1)} %get-tuple-element.45), channel_id=1, source_target_pairs={{8,0},{16,8},{24,16},{32,24},{40,32},{48,40},{56,48},{64,56},{72,6... | collective-permute-start | bytes 98312 | tf_op jit(solution)/shard_map/ppermute | solution.py:304
  116.2 2.4 %collective-permute-start.10 = (bf16[2,32,128]{2,1,0:T(8,128)(2,1)S(1)}, bf16[2,32,128]{2,1,0:T(8,128)(2,1)S(1)}, u32[]{:S(2)}, u32[]{:S(2)}) collective-permute-start(bf16[2,32,128]{2,1,0:T(8,128)(2,1)S(1)} %get-tuple-element.46), channel_id=1, source_target_pairs={{0,4},{4,0},{1,5},{5,1},{2,6},{6,2},{3,7},{7,3},{8,12},{12,8},{9,1... | collective-permute-start | bytes 49160 | tf_op jit(solution)/shard_map/ppermute | solution.py:305
  118.6 1.7 %collective-permute-done.10.xsp = bf16[2,32,128]{2,1,0:T(8,128)(2,1)S(1)} collective-permute-done((bf16[2,32,128]{2,1,0:T(8,128)(2,1)S(1)}, bf16[2,32,128]{2,1,0:T(8,128)(2,1)S(1)}, u32[]{:S(2)}, u32[]{:S(2)}) %collective-permute-start.10) | collective-permute-done | bytes 16416 | tf_op jit(solution)/shard_map/ppermute | solution.py:305
  120.4 5.1 %shard_map.65 = f32[2048,128]{1,0:T(8,128)} custom-call(f32[64,32,128]{2,1,0:T(8,128)S(1)} %get-tuple-element.43.xs, f32[2048,128]{1,0:T(8,128)S(1)} %bitcast.9, f32[2048,128]{1,0:T(8,128)S(1)} %bitcast.7, f32[1,32]{1,0:T(1,128)S(1)} %bitcast.11, f32[64,128]{1,0:T(8,128)S(1)} %collective-permute-done.8.xdn, f32[64,128]{1,0:T(8,128)S(1)} %collective-permute-done.9.xup, ...), custom_call_target="tpu_custom_call" | custom-call | flops 10000000 | bytes 4000000 | tf_op jit(solution)/shard_map/pallas_call | solution.py:373
  (36 shorter events, 3.9 us)
Async XLA Ops:
  0.6 1.2 copy-start.1
  6.6 51.2 %copy-start = (bf16[1024,1024]{1,0:T(8,128)(2,1)S(1)}, bf16[1024,1024]{1,0:T(8,128)(2,1)}, u32[]{:S(2)}) copy-start(bf16[1024,1024]{1,0:T(8,128)(2,1)} %line.5) | copy-start | bytes 6291460
  49.7 8.9 %collective-permute-start = (bf16[32,1024]{1,0:T(8,128)(2,1)S(1)}, bf16[32,1024]{1,0:T(8,128)(2,1)S(1)}, u32[]{:S(2)}, u32[]{:S(2)}) collective-permute-start(bf16[32,1024]{1,0:T(8,128)(2,1)S(1)} %get-tuple-element.31), channel_id=1, source_target_pairs={{0,64},{1,65},{2,66},{3,67},{4,68},{5,69},{6,70},{7,71},{8,72},{9,... | collective-permute-start | bytes 196616 | tf_op jit(solution)/shard_map/ppermute | solution.py:323
  50.1 8.5 %collective-permute-start.1 = (bf16[32,1024]{1,0:T(8,128)(2,1)S(1)}, bf16[32,1024]{1,0:T(8,128)(2,1)S(1)}, u32[]{:S(2)}, u32[]{:S(2)}) collective-permute-start(bf16[32,1024]{1,0:T(8,128)(2,1)S(1)} %get-tuple-element.32), channel_id=1, source_target_pairs={{0,196},{1,197},{2,198},{3,199},{4,192},{5,193},{6,194},{7,195},{8... | collective-permute-start | bytes 196616 | tf_op jit(solution)/shard_map/ppermute | solution.py:323
  54.9 4.9 %collective-permute-start.2 = (bf16[32,1024]{1,0:T(8,128)(2,1)S(1)}, bf16[32,1024]{1,0:T(8,128)(2,1)S(1)}, u32[]{:S(2)}, u32[]{:S(2)}) collective-permute-start(bf16[32,1024]{1,0:T(8,128)(2,1)S(1)} %get-tuple-element.33), channel_id=1, source_target_pairs={{0,8},{1,9},{2,10},{3,11},{4,12},{5,13},{6,14},{7,15},{8,16},{9,17... | collective-permute-start | bytes 196616 | tf_op jit(solution)/shard_map/ppermute | solution.py:323
  55.3 4.4 %collective-permute-start.3 = (bf16[32,1024]{1,0:T(8,128)(2,1)S(1)}, bf16[32,1024]{1,0:T(8,128)(2,1)S(1)}, u32[]{:S(2)}, u32[]{:S(2)}) collective-permute-start(bf16[32,1024]{1,0:T(8,128)(2,1)S(1)} %get-tuple-element.34), channel_id=1, source_target_pairs={{0,59},{1,56},{2,57},{3,58},{4,63},{5,60},{6,61},{7,62},{8,0},{9,1... | collective-permute-start | bytes 196616 | tf_op jit(solution)/shard_map/ppermute | solution.py:323
  64.5 8.7 %collective-permute-start.4 = (f32[16,1024]{1,0:T(8,128)S(1)}, f32[16,1024]{1,0:T(8,128)S(1)}, u32[]{:S(2)}, u32[]{:S(2)}) collective-permute-start(f32[16,1024]{1,0:T(8,128)S(1)} %get-tuple-element.38), channel_id=1, source_target_pairs={{0,64},{1,65},{2,66},{3,67},{4,68},{5,69},{6,70},{7,71},{8,72},{9,... | collective-permute-start | bytes 196616 | tf_op jit(solution)/shard_map/ppermute | solution.py:323
  64.6 8.6 %collective-permute-start.5 = (f32[16,1024]{1,0:T(8,128)S(1)}, f32[16,1024]{1,0:T(8,128)S(1)}, u32[]{:S(2)}, u32[]{:S(2)}) collective-permute-start(f32[16,1024]{1,0:T(8,128)S(1)} %get-tuple-element.39), channel_id=1, source_target_pairs={{0,196},{1,197},{2,198},{3,199},{4,192},{5,193},{6,194},{7,195},{8... | collective-permute-start | bytes 196616 | tf_op jit(solution)/shard_map/ppermute | solution.py:323
  69.7 5.8 %collective-permute-start.6 = (f32[16,1024]{1,0:T(8,128)S(1)}, f32[16,1024]{1,0:T(8,128)S(1)}, u32[]{:S(2)}, u32[]{:S(2)}) collective-permute-start(f32[16,1024]{1,0:T(8,128)S(1)} %get-tuple-element.40), channel_id=1, source_target_pairs={{0,8},{1,9},{2,10},{3,11},{4,12},{5,13},{6,14},{7,15},{8,16},{9,17... | collective-permute-start | bytes 196616 | tf_op jit(solution)/shard_map/ppermute | solution.py:323
  69.7 5.8 %collective-permute-start.7 = (f32[16,1024]{1,0:T(8,128)S(1)}, f32[16,1024]{1,0:T(8,128)S(1)}, u32[]{:S(2)}, u32[]{:S(2)}) collective-permute-start(f32[16,1024]{1,0:T(8,128)S(1)} %get-tuple-element.41), channel_id=1, source_target_pairs={{0,59},{1,56},{2,57},{3,58},{4,63},{5,60},{6,61},{7,62},{8,0},{9,1... | collective-permute-start | bytes 196616 | tf_op jit(solution)/shard_map/ppermute | solution.py:323
  75.5 44.9 %copy-start.4 = (f32[32,64,128]{2,1,0:T(8,128)S(1)}, f32[32,64,128]{2,1,0:T(8,128)}, u32[]{:S(2)}) copy-start(f32[32,64,128]{2,1,0:T(8,128)} %param.5) | copy-start | bytes 3145732
  80.3 40.0 %copy-start.2 = (f32[32,64,128]{2,1,0:T(8,128)S(1)}, f32[32,64,128]{2,1,0:T(8,128)}, u32[]{:S(2)}) copy-start(f32[32,64,128]{2,1,0:T(8,128)} %param.4) | copy-start | bytes 3145732
  80.3 40.0 %copy-start.6 = (f32[32]{0:T(128)S(1)}, f32[32]{0:T(128)}, u32[]{:S(2)}) copy-start(f32[32]{0:T(128)} %param.6) | copy-start | bytes 388
  80.3 26.8 %all-to-all-start.1 = ((bf16[32,32,256]{2,1,0:T(8,128)(2,1)}), bf16[32,32,256]{2,1,0:T(8,128)(2,1)S(1)}, u32[]{:S(2)}, u32[]{:S(2)}) async-start(bf16[32,32,256]{2,1,0:T(8,128)(2,1)} %bitcast.3), calls=%async_computation.1 | async-start | bytes 1048576 | tf_op jit(solution)/shard_map/all_to_all | solution.py:366
  89.9 24.9 %collective-permute-start.16 = (bf16[8,32,128]{2,1,0:T(8,128)(2,1)S(1)}, bf16[8,32,128]{2,1,0:T(8,128)(2,1)S(1)}, u32[]{:S(2)}, u32[]{:S(2)}) collective-permute-start(bf16[8,32,128]{2,1,0:T(8,128)(2,1)S(1)} %get-tuple-element.52), channel_id=1, source_target_pairs={{0,1},{1,2},{2,3},{3,0},{4,5},{5,6},{6,7},{7,4},{8,9},{9,10},{10,1... | collective-permute-start | bytes 196616 | tf_op jit(solution)/shard_map/ppermute | solution.py:306
  90.0 20.9 %collective-permute-start.13 = (f32[64,128]{1,0:T(8,128)S(1)}, f32[64,128]{1,0:T(8,128)S(1)}, u32[]{:S(2)}, u32[]{:S(2)}) collective-permute-start(f32[64,128]{1,0:T(8,128)S(1)} %get-tuple-element.49), channel_id=1, source_target_pairs={{0,8},{8,16},{16,24},{24,32},{32,40},{40,48},{48,56},{56,64},{64,7... | collective-permute-start | bytes 98312 | tf_op jit(solution)/shard_map/ppermute | solution.py:303
  93.2 23.0 %collective-permute-start.17 = (bf16[8,32,128]{2,1,0:T(8,128)(2,1)S(1)}, bf16[8,32,128]{2,1,0:T(8,128)(2,1)S(1)}, u32[]{:S(2)}, u32[]{:S(2)}) collective-permute-start(bf16[8,32,128]{2,1,0:T(8,128)(2,1)S(1)} %get-tuple-element.53), channel_id=1, source_target_pairs={{1,0},{2,1},{3,2},{0,3},{5,4},{6,5},{7,6},{4,7},{9,8},{10,9},{11,1... | collective-permute-start | bytes 196616 | tf_op jit(solution)/shard_map/ppermute | solution.py:307
  94.0 16.2 %collective-permute-start.15 = (bf16[2,32,128]{2,1,0:T(8,128)(2,1)S(1)}, bf16[2,32,128]{2,1,0:T(8,128)(2,1)S(1)}, u32[]{:S(2)}, u32[]{:S(2)}) collective-permute-start(bf16[2,32,128]{2,1,0:T(8,128)(2,1)S(1)} %get-tuple-element.51), channel_id=1, source_target_pairs={{0,4},{4,0},{1,5},{5,1},{2,6},{6,2},{3,7},{7,3},{8,12},{12,8},{9,1... | collective-permute-start | bytes 49160 | tf_op jit(solution)/shard_map/ppermute | solution.py:305
  96.5 14.4 %collective-permute-start.14 = (f32[64,128]{1,0:T(8,128)S(1)}, f32[64,128]{1,0:T(8,128)S(1)}, u32[]{:S(2)}, u32[]{:S(2)}) collective-permute-start(f32[64,128]{1,0:T(8,128)S(1)} %get-tuple-element.50), channel_id=1, source_target_pairs={{8,0},{16,8},{24,16},{32,24},{40,32},{48,40},{56,48},{64,56},{72,6... | collective-permute-start | bytes 98312 | tf_op jit(solution)/shard_map/ppermute | solution.py:304
  110.2 10.2 %collective-permute-start.11 = (bf16[8,32,128]{2,1,0:T(8,128)(2,1)S(1)}, bf16[8,32,128]{2,1,0:T(8,128)(2,1)S(1)}, u32[]{:S(2)}, u32[]{:S(2)}) collective-permute-start(bf16[8,32,128]{2,1,0:T(8,128)(2,1)S(1)} %get-tuple-element.47), channel_id=1, source_target_pairs={{0,1},{1,2},{2,3},{3,0},{4,5},{5,6},{6,7},{7,4},{8,9},{9,10},{10,1... | collective-permute-start | bytes 196616 | tf_op jit(solution)/shard_map/ppermute | solution.py:306
  110.9 9.5 %collective-permute-start.12 = (bf16[8,32,128]{2,1,0:T(8,128)(2,1)S(1)}, bf16[8,32,128]{2,1,0:T(8,128)(2,1)S(1)}, u32[]{:S(2)}, u32[]{:S(2)}) collective-permute-start(bf16[8,32,128]{2,1,0:T(8,128)(2,1)S(1)} %get-tuple-element.48), channel_id=1, source_target_pairs={{1,0},{2,1},{3,2},{0,3},{5,4},{6,5},{7,6},{4,7},{9,8},{10,9},{11,1... | collective-permute-start | bytes 196616 | tf_op jit(solution)/shard_map/ppermute | solution.py:307
  110.9 9.4 %collective-permute-start.8 = (f32[64,128]{1,0:T(8,128)S(1)}, f32[64,128]{1,0:T(8,128)S(1)}, u32[]{:S(2)}, u32[]{:S(2)}) collective-permute-start(f32[64,128]{1,0:T(8,128)S(1)} %get-tuple-element.44), channel_id=1, source_target_pairs={{0,8},{8,16},{16,24},{24,32},{32,40},{40,48},{48,56},{56,64},{64,7... | collective-permute-start | bytes 98312 | tf_op jit(solution)/shard_map/ppermute | solution.py:303
  114.8 5.5 %collective-permute-start.9 = (f32[64,128]{1,0:T(8,128)S(1)}, f32[64,128]{1,0:T(8,128)S(1)}, u32[]{:S(2)}, u32[]{:S(2)}) collective-permute-start(f32[64,128]{1,0:T(8,128)S(1)} %get-tuple-element.45), channel_id=1, source_target_pairs={{8,0},{16,8},{24,16},{32,24},{40,32},{48,40},{56,48},{64,56},{72,6... | collective-permute-start | bytes 98312 | tf_op jit(solution)/shard_map/ppermute | solution.py:304
  116.2 4.2 %collective-permute-start.10 = (bf16[2,32,128]{2,1,0:T(8,128)(2,1)S(1)}, bf16[2,32,128]{2,1,0:T(8,128)(2,1)S(1)}, u32[]{:S(2)}, u32[]{:S(2)}) collective-permute-start(bf16[2,32,128]{2,1,0:T(8,128)(2,1)S(1)} %get-tuple-element.46), channel_id=1, source_target_pairs={{0,4},{4,0},{1,5},{5,1},{2,6},{6,2},{3,7},{7,3},{8,12},{12,8},{9,1... | collective-permute-start | bytes 49160 | tf_op jit(solution)/shard_map/ppermute | solution.py:305
  (2 other events, 1.9 us)
where the time goes:
time: 128 us; the launch traced here: 125 us
  starting transfers between devices  42.5 us (33%)
  blocking collectives  42.4 us (33%)
  Pallas kernels  22 us (17%)
  waiting for transfers between devices  14.6 us (11%)
  local copies, waits for them, and re-layouts  3.12 us (2%)
    all_to_all x1, blocking collectives, body(): recv = lax.all_to_all(send, 'wall', 0, 0, tiled=True)  42.4 us
    ppermute x8, starting transfers between devices, line_shift(): return lax.ppermute(value, ('wall', 'span', 'stream'), pairs)  16.8 us
    all_to_all x1, starting transfers between devices, body(): lax.all_to_all(send.reshape(WY * WZ, ROWS, CELLS), 'wall', 0, 0, tiled=True)  9.59 us
    all_to_all x1, waiting for transfers between devices, body(): lax.all_to_all(send.reshape(WY * WZ, ROWS, CELLS), 'wall', 0, 0, tiled=True)  9.43 us
    ppermute x2, starting transfers between devices, block_edges(): lax.ppermute(ew1, 'wall', rising)  7.06 us
    pallas_call x1, Pallas kernels, body(): call(last_resid, shape((ROWS * SPAN, LANES), F32), (tall, tall))  5.06 us
    ppermute x2, starting transfers between devices, block_edges(): lax.ppermute(es, 'span', [(0, 1), (1, 0)])  4.89 us
    pallas_call x1, Pallas kernels, body(): call(third_step, shape((NW, CELLS), BF16), (ext, ext, rounded, pltpu.VMEM...  4.87 us
  transfers between devices with their start and end apart: 19, of which 4 were waited for; matrix products, arithmetic and copies ran while one was open for 0% of the time, Pallas kernels for 3%

commit v1 on v0

--- a/solution.py
+++ b/solution.py
@@ -15,7 +15,6 @@
 TAIL = 8
 MID = 0.5
 F32, BF16 = jnp.float32, jnp.bfloat16
-VMEM = pl.BlockSpec(memory_space=pltpu.VMEM)
 PARAMS = pltpu.CompilerParams(vmem_limit_bytes=40 * 1024 * 1024)
 
 
@@ -41,15 +40,14 @@
     return jax.ShapeDtypeStruct(dims, dtype)
 
 
-def call(kernel, outs, scratch=(), **cost):
+def call(kernel, outs, scratch=(), **specs):
     return pl.pallas_call(
         kernel,
         out_shape=outs,
         scratch_shapes=list(scratch),
         compiler_params=PARAMS,
-        cost_estimate=pl.CostEstimate(
-            flops=cost.get("flops", 10**7), bytes_accessed=cost.get("size", 4 * 10**6), transcendentals=0
-        ),
+        cost_estimate=pl.CostEstimate(flops=10**7, bytes_accessed=4 * 10**6, transcendentals=0),
+        **specs,
     )
 
 
@@ -72,7 +70,24 @@
     return pl.ds(s, ROWS, stride=SPAN)
 
 
-def pack(b_ref, v_ref, m_ref, send, ew0, ew1, es, exl, exr):
+def edge_lanes(sides, offset):
+    at = lax.broadcasted_iota(jnp.int32, (8 * LANES, LANES), 0)
+    to = lax.broadcasted_iota(jnp.int32, (8 * LANES, LANES), 1)
+    out = []
+    for lanes, pick in sides:
+        chosen = (at % BX == pick) & (to == at // BX + offset)
+        one = jnp.where(chosen, 1.0, 0.0).astype(BF16)
+        out.append(jnp.dot(lanes, one, preferred_element_type=F32).astype(BF16))
+    return out
+
+
+def pack(b_hbm, v_hbm, m_ref, send, es, dl, dr, b_buf, v_buf, cl, cr, sems):
+    copies = []
+    for t in range(WY):
+        cells = (slice(None), slice(BS * t, BS * (t + 1)), slice(None))
+        for k, (src, dst) in enumerate(((b_hbm, b_buf), (v_hbm, v_buf))):
+            copies.append(pltpu.make_async_copy(src.at[cells], dst.at[cells], sems.at[k, t]))
+            copies[-1].start()
     m = m_ref[...]
     rest = m
     parts = []
@@ -84,23 +99,38 @@
     tail = jnp.concatenate([tail, jnp.zeros((TAIL, LANES - ROWS), F32)], axis=1).astype(BF16)
     for k in range(WY * WZ):
         send[k, 4 * ROWS :, :] = tail
+    flat = [buf.reshape(ROWS * SPAN, LANES) for buf in (b_buf, v_buf)]
     for t in range(WY):
-        for g in range(2):
-            for ref, off, mid in ((b_ref, 0, 0.0), (v_ref, 2, MID)):
-                parts = lane_blocks([ref[strided(16 * t + 8 * g + i), :] - mid for i in range(8)])
-                rows = slice(ROWS * (off + g), ROWS * (off + g + 1))
+        for k, mid in enumerate((0.0, MID)):
+            copies[2 * t + k].wait()
+            for g in range(2):
+                parts = lane_blocks([flat[k][strided(16 * t + 8 * g + i), :] - mid for i in range(8)])
+                rows = slice(ROWS * (2 * k + g), ROWS * (2 * k + g + 1))
                 for z in range(WZ):
                     send[WZ * t + z, rows, :] = parts[z].astype(BF16)
-                if off:
-                    exl[2 * t + g] = parts[0].astype(BF16)
-                    exr[2 * t + g] = parts[7].astype(BF16)
-    ew0[...] = v_ref[0:SPAN, :] * m[:, :1]
-    ew1[...] = v_ref[(ROWS - 1) * SPAN :, :] * m[:, ROWS - 1 :]
-    es[0] = (v_ref[strided(0), :] - MID).astype(BF16)
-    es[1] = (v_ref[strided(SPAN - 1), :] - MID).astype(BF16)
-
-
-def to_lines(recv, bt, vt, metric, *edges):
+                if k:
+                    lanes = slice(LANES * (2 * t + g), LANES * (2 * t + g + 1))
+                    cl[:, lanes] = parts[0].astype(BF16)
+                    cr[:, lanes] = parts[7].astype(BF16)
+    es[0] = (flat[1][strided(0), :] - MID).astype(BF16)
+    es[1] = (flat[1][strided(SPAN - 1), :] - MID).astype(BF16)
+    dl[...], dr[...] = edge_lanes(((cl[...], 0), (cr[...], BX - 1)), SPAN)
+
+
+def to_lines(recv, bt, vt, metric, ends, *edges):
+    count = WY * WZ
+    nothing = jnp.zeros((1, LANES), F32)
+    for k in range(count):
+        rows = []
+        for other, at in ((k - 1, ROWS - 1), (k + 1, 0)):
+            if not 0 <= other < count:
+                rows += [nothing] * 2
+                continue
+            m = jnp.sum(recv[other, 4 * ROWS :, :].astype(F32), axis=0, keepdims=True)
+            for g in range(2):
+                v = recv[other, ROWS * (2 + g) : ROWS * (3 + g), :].astype(F32) + MID
+                rows.append(v[at : at + 1] * m[:, at : at + 1])
+        ends[k] = jnp.concatenate(rows, axis=0)
     for i in range(8):
         row = jnp.zeros((TAIL, LANES), F32)
         for j in range(4):
@@ -192,14 +222,16 @@
     d2[...] = keep * x1[...] + scale * apply_lines(rt[...], line[...])
     x2[...] = x1[...] + d2[...]
     grid = x2[...].reshape(BS, BX, NW)
-    e0[...] = grid[0]
-    e1[...] = grid[BS - 1]
-    e2[...] = grid[:, 0, :]
-    e3[...] = grid[:, BX - 1, :]
-
-
-def third_step(x2, d2, bt, vt, su, sd, xl, xr, vsu, vsd, vxl, vxr, line, metric, send, xe, ve, rt, x3):
-    fill(xe, x2[...].reshape(BS, BX, NW), su[...], sd[...], xl[...], xr[...])
+    e0[...] = grid[0].astype(BF16)
+    e1[...] = grid[BS - 1].astype(BF16)
+    e2[...] = grid[:, 0, :].astype(BF16)
+    e3[...] = grid[:, BX - 1, :].astype(BF16)
+
+
+def third_step(
+    x2, d2, bt, vt, su, sd, xl, xr, vsu, vsd, vxl, vxr, line, metric, ends, send, xe, ve, rt, x3
+):
+    fill(xe, x2[...].reshape(BS, BX, NW), *(ref[...].astype(F32) for ref in (su, sd, xl, xr)))
     fill(
         ve,
         vt[...].astype(F32).reshape(BS, BX, NW) + MID,
@@ -213,98 +245,107 @@
     lax.fori_loop(0, BS, one, 0)
     keep, scale = WEIGHTS[2]
     x3[...] = x2[...] + keep * d2[...] + scale * apply_lines(rt[...], line[...])
+    count = WY * WZ
+    nothing = jnp.zeros((1, LANES), F32)
+    firsts, lasts = {}, {}
     for j in range(2):
         for i in range(8):
             tile = x3[j * LANES : (j + 1) * LANES, i * LANES : (i + 1) * LANES].T
-            send[i * LANES : (i + 1) * LANES, j * LANES : (j + 1) * LANES] = tile.astype(BF16)
-
-
-def unpack(recv, x3, xs, ew0, ew1, es, exl, exr):
+            for k in range(4):
+                part = tile[ROWS * k : ROWS * (k + 1)]
+                send[4 * i + k, ROWS * j : ROWS * (j + 1), :] = part.astype(BF16)
+                firsts[4 * i + k, j] = part[:1]
+                lasts[4 * i + k, j] = part[ROWS - 1 :]
+    for k in range(count):
+        rows = [lasts.get((k - 1, j), nothing) for j in range(2)]
+        rows += [firsts.get((k + 1, j), nothing) for j in range(2)]
+        send[k, 2 * ROWS :, :] = jnp.concatenate(rows + [ends[k]], axis=0).astype(BF16)
+
+
+def unpack(recv, ves, vdl, vdr, xs, beyond, es, dl, dr, cl, cr):
     for t in range(WY):
         for g in range(2):
-            lanes = slice(LANES * g, LANES * (g + 1))
-            parts = [recv[WZ * t + z, :, lanes] for z in range(WZ)]
-            exl[2 * t + g] = parts[0]
-            exr[2 * t + g] = parts[7]
+            rows = slice(ROWS * g, ROWS * (g + 1))
+            parts = [recv[WZ * t + z, rows, :] for z in range(WZ)]
+            lanes = slice(LANES * (2 * t + g), LANES * (2 * t + g + 1))
+            cl[:, lanes] = parts[0]
+            cr[:, lanes] = parts[7]
             parts = lane_blocks([p.astype(F32) for p in parts])
             for i in range(8):
-                s = 16 * t + 8 * g + i
-                x3[strided(s), :] = parts[i]
-                xs[s] = parts[i]
-    ew0[...] = x3[0:SPAN, :]
-    ew1[...] = x3[(ROWS - 1) * SPAN :, :]
+                xs[16 * t + 8 * g + i] = parts[i]
+        parts = lane_blocks([recv[WZ * t + z, 2 * ROWS :, :].astype(F32) for z in range(WZ)])
+        for i in range(8):
+            beyond[t, i] = parts[i]
     es[0] = xs[0].astype(BF16)
     es[1] = xs[SPAN - 1].astype(BF16)
+    es[2] = ves[0]
+    es[3] = ves[1]
+    left, right = edge_lanes(((cl[...], 0), (cr[...], BX - 1)), 0)
+    dl[...] = left + vdl[...]
+    dr[...] = right + vdr[...]
 
 
 def last_resid(
-    xs, v_ref, b_ref, m_ref, xdn, xup, xsp, xlf, xrt, kdn, kup, vsp, vlf, vrt, out, xe, ve
+    xs, v_ref, b_ref, m_ref, beyond, spans, lefts, rights, x3, out, xe, ve, x_buf, r_buf, sems
 ):
     xe[1 : SPAN + 1] = xs[...]
-    xe[0] = xsp[1].astype(F32)
-    xe[SPAN + 1] = xsp[0].astype(F32)
+    xe[0] = spans[1].astype(F32)
+    xe[SPAN + 1] = spans[0].astype(F32)
     for s in range(SPAN):
         ve[s + 1] = v_ref[strided(s), :]
-    ve[0] = vsp[1].astype(F32) + MID
-    ve[SPAN + 1] = vsp[0].astype(F32) + MID
+    ve[0] = spans[3].astype(F32) + MID
+    ve[SPAN + 1] = spans[2].astype(F32) + MID
     row = lax.broadcasted_iota(jnp.int32, (ROWS, LANES), 0)
     lane = lax.broadcasted_iota(jnp.int32, (ROWS, LANES), 1)
     square = lax.broadcasted_iota(jnp.int32, (ROWS, ROWS), 0)
     square = square == lax.broadcasted_iota(jnp.int32, (ROWS, ROWS), 1)
     m = jnp.sum(jnp.where(square, m_ref[...], 0.0), axis=1, keepdims=True)
-
-    def eight(q, _):
-        rows = pl.ds(pl.multiple_of(8 * q, 8), 8)
-        beyond = [ref[rows, :] for ref in (xdn, xup, kdn, kup)]
-        for i in range(8):
-            s = 8 * q + i
-            xc, vc = xe[s + 1], ve[s + 1]
-            total = (vc + ve[s]) * (xc - xe[s]) + (vc + ve[s + 2]) * (xc - xe[s + 2])
-            xb, xa, kb, ka = (block[i : i + 1] for block in beyond)
-            xn = jnp.where(row == 0, xb, pltpu.roll(xc, 1, 0))
-            kc = m * vc
-            kn = jnp.where(row == 0, kb, pltpu.roll(kc, 1, 0))
-            total += (kc + kn) * (xc - xn)
-            xn = jnp.where(row == ROWS - 1, xa, pltpu.roll(xc, ROWS - 1, 0))
-            kn = jnp.where(row == ROWS - 1, ka, pltpu.roll(kc, ROWS - 1, 0))
-            total += (kc + kn) * (xc - xn)
-            left = (LANES - (BX * i + BX - 1)) % LANES
-            xn = jnp.where(lane == 0, pltpu.roll(xlf[q].astype(F32), left, 1), pltpu.roll(xc, 1, 1))
-            vn = jnp.where(
-                lane == 0, pltpu.roll(vlf[q].astype(F32) + MID, left, 1), pltpu.roll(vc, 1, 1)
-            )
-            total += (vc + vn) * (xc - xn)
-            right = LANES - 1 - BX * i
-            xn = jnp.where(
-                lane == LANES - 1,
-                pltpu.roll(xrt[q].astype(F32), right, 1),
-                pltpu.roll(xc, LANES - 1, 1),
-            )
-            vn = jnp.where(
-                lane == LANES - 1,
-                pltpu.roll(vrt[q].astype(F32) + MID, right, 1),
-                pltpu.roll(vc, LANES - 1, 1),
-            )
-            total += (vc + vn) * (xc - xn)
-            out[strided(s), :] = b_ref[strided(s), :] - (xc + 0.5 * total)
-        return 0
-
-    lax.fori_loop(0, SPAN // 8, eight, 0)
-
-
-def block_edges(ew0, ew1, es, exl, exr):
-    walls = lax.axis_size("wall")
+    near_left = lefts[...].astype(F32)
+    near_right = rights[...].astype(F32)
+    x_flat = x_buf.reshape(ROWS * SPAN, LANES)
+    r_flat = r_buf.reshape(ROWS * SPAN, LANES)
+    copies = []
+    for t in range(WY):
+        for g in range(2):
+            for i in range(8):
+                s = 16 * t + 8 * g + i
+                xc, vc = xe[s + 1], ve[s + 1]
+                x_flat[strided(s), :] = xc
+                total = (vc + ve[s]) * (xc - xe[s]) + (vc + ve[s + 2]) * (xc - xe[s + 2])
+                edge = beyond[t, i]
+                xb, xa, kb, ka = (edge[2 * k + g : 2 * k + g + 1] for k in range(4))
+                kc = m * vc
+                xn = jnp.where(row == 0, xb, pltpu.roll(xc, 1, 0))
+                kn = jnp.where(row == 0, kb, pltpu.roll(kc, 1, 0))
+                total += (kc + kn) * (xc - xn)
+                xn = jnp.where(row == ROWS - 1, xa, pltpu.roll(xc, ROWS - 1, 0))
+                kn = jnp.where(row == ROWS - 1, ka, pltpu.roll(kc, ROWS - 1, 0))
+                total += (kc + kn) * (xc - xn)
+                xn = jnp.where(lane == 0, near_left[:, s : s + 1], pltpu.roll(xc, 1, 1))
+                vn = near_left[:, SPAN + s : SPAN + s + 1] + MID
+                vn = jnp.where(lane == 0, vn, pltpu.roll(vc, 1, 1))
+                total += (vc + vn) * (xc - xn)
+                xn = jnp.where(lane == LANES - 1, near_right[:, s : s + 1], pltpu.roll(xc, LANES - 1, 1))
+                vn = near_right[:, SPAN + s : SPAN + s + 1] + MID
+                vn = jnp.where(lane == LANES - 1, vn, pltpu.roll(vc, LANES - 1, 1))
+                total += (vc + vn) * (xc - xn)
+                r_flat[strided(s), :] = b_ref[strided(s), :] - (xc + 0.5 * total)
+        cells = (slice(None), slice(BS * t, BS * (t + 1)), slice(None))
+        for k, (src, dst) in enumerate(((x_buf, x3), (r_buf, out))):
+            copies.append(pltpu.make_async_copy(src.at[cells], dst.at[cells], sems.at[k, t]))
+            copies[-1].start()
+    for copy in copies:
+        copy.wait()
+
+
+def block_edges(es, dl, dr):
     streams = lax.axis_size("stream")
-    rising = [(i, i + 1) for i in range(walls - 1)]
-    falling = [(i + 1, i) for i in range(walls - 1)]
     right = [(i, (i + 1) % streams) for i in range(streams)]
     left = [((i + 1) % streams, i) for i in range(streams)]
     return (
-        lax.ppermute(ew1, "wall", rising),
-        lax.ppermute(ew0, "wall", falling),
         lax.ppermute(es, "span", [(0, 1), (1, 0)]),
-        lax.ppermute(exr, "stream", right),
-        lax.ppermute(exl, "stream", left),
+        lax.ppermute(dr, "stream", right),
+        lax.ppermute(dl, "stream", left),
     )
 
 
@@ -336,16 +377,28 @@
     b = right_side.reshape(ROWS * SPAN, LANES)
     v = viscosity.reshape(ROWS * SPAN, LANES)
     m = wall_metric.reshape(1, ROWS)
-    chunk = shape((2 * WY, ROWS, LANES), BF16)
-    wide = shape((SPAN, LANES), F32)
-    deep = shape((2, ROWS, LANES), BF16)
-    block_outs = (wide, wide, deep, chunk, chunk)
-    send, *edges = call(pack, (shape((WY * WZ, 4 * ROWS + TAIL, LANES), BF16), *block_outs))(b, v, m)
-    v_edges = block_edges(*edges)
+    block = pltpu.VMEM((ROWS, SPAN, LANES), F32)
+    sems = pltpu.SemaphoreType.DMA((2, WY))
+    side = pltpu.VMEM((ROWS, 8 * LANES), BF16)
+    dense = shape((ROWS, LANES), BF16)
+    hbm, vmem = pl.BlockSpec(memory_space=pltpu.HBM), pl.BlockSpec(memory_space=pltpu.VMEM)
+    send, *v_edges = call(
+        pack,
+        (
+            shape((WY * WZ, 4 * ROWS + TAIL, LANES), BF16),
+            shape((2, ROWS, LANES), BF16),
+            dense,
+            dense,
+        ),
+        (block, block, side, side, sems),
+        in_specs=(hbm, hbm, vmem),
+    )(right_side, viscosity, m)
     recv = lax.all_to_all(send, "wall", 0, 0, tiled=True)
     lines = shape((CELLS, NW), BF16)
-    bt, vt, metric, *edges = call(
-        to_lines, (lines, lines, shape((1, NW), F32)) + (shape((2 * BX, NW), BF16),) * 4
+    bt, vt, metric, ends, *edges = call(
+        to_lines,
+        (lines, lines, shape((1, NW), F32), shape((WY * WZ, 4, LANES), F32))
+        + (shape((2 * BX, NW), BF16),) * 4,
     )(recv)
     near = line_edges(*edges)
     x1 = call(first_lines, shape((CELLS, NW), F32))(bt, line_inverse)
@@ -354,27 +407,36 @@
     rounded = pltpu.VMEM((CELLS, NW), BF16)
     x2, d2, *edges = call(
         second_step,
-        (field, field) + (shape((BX, NW), F32),) * 4,
+        (field, field) + (shape((BX, NW), BF16),) * 4,
         (ext, ext, rounded, pltpu.VMEM((4 * BX, NW), BF16)),
     )(x1, bt, vt, *near, line_inverse, metric)
     x_near = line_edges(*edges)
     send = call(
         third_step,
-        shape((NW, CELLS), BF16),
+        shape((WY * WZ, 2 * ROWS + TAIL, LANES), BF16),
         (ext, ext, rounded, pltpu.VMEM((CELLS, NW), F32)),
-    )(x2, d2, bt, vt, *x_near, *near, line_inverse, metric)
-    recv = lax.all_to_all(send.reshape(WY * WZ, ROWS, CELLS), "wall", 0, 0, tiled=True)
-    x3, xs, *edges = call(
+    )(x2, d2, bt, vt, *x_near, *near, line_inverse, metric, ends)
+    recv = lax.all_to_all(send, "wall", 0, 0, tiled=True)
+    xs, beyond, *edges = call(
         unpack,
-        (shape((ROWS * SPAN, LANES), F32), shape((SPAN, ROWS, LANES), F32), *block_outs),
-    )(recv)
+        (
+            shape((SPAN, ROWS, LANES), F32),
+            shape((WY, 8, TAIL, LANES), F32),
+            shape((4, ROWS, LANES), BF16),
+            dense,
+            dense,
+        ),
+        (side, side),
+    )(recv, *v_edges)
     x_edges = block_edges(*edges)
     tall = pltpu.VMEM((SPAN + 2, ROWS, LANES), F32)
-    residual = call(last_resid, shape((ROWS * SPAN, LANES), F32), (tall, tall))(
-        xs, v, b, m, *x_edges, *v_edges
-    )
-    dims = right_side.shape
-    return x3.reshape(dims), residual.reshape(dims)
+    whole = shape(right_side.shape, F32)
+    return call(
+        last_resid,
+        (whole, whole),
+        (tall, tall, block, block, sems),
+        out_specs=(hbm, hbm),
+    )(xs, v, b, m, beyond, *x_edges)
 
 
 def solution(mesh):

time: 128 us -> 120 us (0.938); the launches traced: 125 us -> 119 us
  blocking collectives: 42.4 us -> 69.7 us
  starting transfers between devices: 42.5 us -> 18.9 us
  waiting for transfers between devices: 14.6 us -> 5.93 us
  Pallas kernels: 22 us -> 20.6 us
    all_to_all x1 -> x2, blocking collectives: 42.4 us -> 69.7 us  [body(): recv = lax.all_to_all(send, 'wall', 0, 0, tiled=True)]
    ppermute x8 -> x2, starting transfers between devices: 11.3 us -> 0.51 us  [the longest x1 0.51 us: block_edges(): lax.ppermute(dl, 'stream', left)]
    all_to_all x1 -> x0, starting transfers between devices: 9.59 us -> none  [body(): lax.all_to_all(send.reshape(WY * WZ, ROWS, CELLS), 'wall', 0, 0, tiled=True)]
    all_to_all x1 -> x0, waiting for transfers between devices: 9.43 us -> none  [body(): lax.all_to_all(send.reshape(WY * WZ, ROWS, CELLS), 'wall', 0, 0, tiled=True)]
    ppermute x2 -> x1, starting transfers between devices: 4.89 us -> 1.62 us  [block_edges(): lax.ppermute(es, 'span', [(0, 1), (1, 0)])]
    ppermute x8 -> x2, waiting for transfers between devices: 0.02 us -> 2.86 us  [the longest x1 2.2 us: block_edges(): lax.ppermute(dl, 'stream', left)]
    ppermute x2 -> x1, waiting for transfers between devices: 1.74 us -> 0.01 us  [block_edges(): lax.ppermute(es, 'span', [(0, 1), (1, 0)])]
    pallas_call x6, Pallas kernels: 21.3 us -> 19.9 us  [the longest x1 5.14 us: body(): call(last_resid, (whole, whole), (tall, tall, block, block, sems), out_sp...]
  transfers between devices with their start and end apart: 19 -> 11, of which waited for: 4 -> 4; matrix products, arithmetic and copies ran while one was open for 0% -> 0% of each run, Pallas kernels for 3% -> 1%
where the time goes in v1:
time: 120 us; the launch traced here: 119 us
  blocking collectives  69.7 us (58%)
  Pallas kernels  20.6 us (17%)
  starting transfers between devices  18.9 us (16%)
  waiting for transfers between devices  5.93 us (5%)
  local copies, waits for them, and re-layouts  3.12 us (3%)
    all_to_all x2, blocking collectives, body(): recv = lax.all_to_all(send, 'wall', 0, 0, tiled=True)  69.7 us
    ppermute x8, starting transfers between devices, line_shift(): return lax.ppermute(value, ('wall', 'span', 'stream'), pairs)  16.8 us
    pallas_call x1, Pallas kernels, body(): call(last_resid, (whole, whole), (tall, tall, block, block, sems), out_sp...  5.14 us
    pallas_call x1, Pallas kernels, body(): call(second_step, (field, field) + (shape((BX, NW), BF16),) * 4, (ext, ex...  4.84 us
    pallas_call x1, Pallas kernels, body(): call(third_step, shape((WY * WZ, 2 * ROWS + TAIL, LANES), BF16), (ext, ex...  4.1 us
    pallas_call x1, Pallas kernels, body(): call(pack, (shape((WY * WZ, 4 * ROWS + TAIL, LANES), BF16), shape((2, ROW...  3.51 us
    unnamed x14, local copies, waits for them, and re-layouts  3.12 us
    ppermute x8, waiting for transfers between devices, line_shift(): return lax.ppermute(value, ('wall', 'span', 'stream'), pairs)  3.07 us
  transfers between devices with their start and end apart: 11, of which 4 were waited for; matrix products, arithmetic and copies ran while one was open for 0% of the time, Pallas kernels for 1%

profile of v1, /device:TPU:1, one launch (start us, length us, event | category | flops | bytes accessed | tf_op | source)
XLA Modules:
  0.0 119.2 jit_solution(13868694195463644705)
XLA Ops:
  0.6 1.2 %copy-done.1 = f32[32,64,128]{2,1,0:T(8,128)S(1)} copy-done((f32[32,64,128]{2,1,0:T(8,128)S(1)}, f32[32,64,128]{2,1,0:T(8,128)}, u32[]{:S(2)}) %copy-start.1) | copy-done | bytes 1048600
  1.9 1.2 %copy-done.3 = f32[32,64,128]{2,1,0:T(8,128)S(1)} copy-done((f32[32,64,128]{2,1,0:T(8,128)S(1)}, f32[32,64,128]{2,1,0:T(8,128)}, u32[]{:S(2)}) %copy-start.3) | copy-done | bytes 1048600
  3.1 0.7 copy-done.5
  3.7 3.5 %shard_map.59 = (bf16[32,136,128]{2,1,0:T(8,128)(2,1)S(1)}, bf16[2,32,128]{2,1,0:T(8,128)(2,1)S(1)}, bf16[32,128]{1,0:T(8,128)(2,1)S(1)}, bf16[32,128]{1,0:T(8,128)(2,1)S(1)}) custom-call(f32[32,64,128]{2,1,0:T(8,128)S(1)} %copy-done.1, f32[32,64,128]{2,1,0:T(8,128)S(1)} %copy-done.3, f32[1,32]{1,0:T(1,128)S(1)} %bitcast.5), custom_call_target="tpu_custom_call" | custom-call | flops 10000000 | bytes 4000000 | tf_op jit(solution)/shard_map/pallas_call | solution.py:385
  7.3 42.4 %all_to_all.10.recv = bf16[32,136,128]{2,1,0:T(8,128)(2,1)S(1)} all-to-all(bf16[32,136,128]{2,1,0:T(8,128)(2,1)S(1)} %get-tuple-element.25), channel_id=1, replica_groups=mesh['wall'=32,'span'=2,'stream'=4] {'wall'}, dimensions={0} | all-to-all | bytes 2228224 | tf_op jit(solution)/shard_map/all_to_all | solution.py:396
  49.6 0.8 shard_map.60
  50.4 0.4 collective-permute-start
  50.8 4.8 %collective-permute-start.1 = (bf16[32,1024]{1,0:T(8,128)(2,1)S(1)}, bf16[32,1024]{1,0:T(8,128)(2,1)S(1)}, u32[]{:S(2)}, u32[]{:S(2)}) collective-permute-start(bf16[32,1024]{1,0:T(8,128)(2,1)S(1)} %get-tuple-element.29), channel_id=1, source_target_pairs={{0,196},{1,197},{2,198},{3,199},{4,192},{5,193},{6,194},{7,195},{8... | collective-permute-start | bytes 196616 | tf_op jit(solution)/shard_map/ppermute | solution.py:364
  55.6 0.5 collective-permute-start.2
  56.1 2.5 %collective-permute-start.3 = (bf16[32,1024]{1,0:T(8,128)(2,1)S(1)}, bf16[32,1024]{1,0:T(8,128)(2,1)S(1)}, u32[]{:S(2)}, u32[]{:S(2)}) collective-permute-start(bf16[32,1024]{1,0:T(8,128)(2,1)S(1)} %get-tuple-element.31), channel_id=1, source_target_pairs={{0,59},{1,56},{2,57},{3,58},{4,63},{5,60},{6,61},{7,62},{8,0},{9,1... | collective-permute-start | bytes 196616 | tf_op jit(solution)/shard_map/ppermute | solution.py:364
  58.5 0.7 shard_map.61.x1
  59.3 1.2 collective-permute-done.2.xl.vxl
  60.5 4.8 %shard_map.62 = (f32[256,1024]{1,0:T(8,128)S(1)}, f32[256,1024]{1,0:T(8,128)S(1)}, bf16[16,1024]{1,0:T(8,128)(2,1)S(1)}, bf16[16,1024]{1,0:T(8,128)(2,1)S(1)}, b...) custom-call(f32[256,1024]{1,0:T(8,128)S(1)} %shard_map.61.x1, bf16[256,1024]{1,0:T(8,128)(2,1)S(1)} %get-tuple-element.26.bt, ...), custom_call_target="tpu_custom_call" | custom-call | flops 10000000 | bytes 4000000 | tf_op jit(solution)/shard_map/pallas_call | solution.py:408
  65.4 5.1 %collective-permute-start.5 = (bf16[16,1024]{1,0:T(8,128)(2,1)S(1)}, bf16[16,1024]{1,0:T(8,128)(2,1)S(1)}, u32[]{:S(2)}, u32[]{:S(2)}) collective-permute-start(bf16[16,1024]{1,0:T(8,128)(2,1)S(1)} %get-tuple-element.36), channel_id=1, source_target_pairs={{0,196},{1,197},{2,198},{3,199},{4,192},{5,193},{6,194},{7,195},{8... | collective-permute-start | bytes 98312 | tf_op jit(solution)/shard_map/ppermute | solution.py:364
  70.5 3.5 %collective-permute-start.7 = (bf16[16,1024]{1,0:T(8,128)(2,1)S(1)}, bf16[16,1024]{1,0:T(8,128)(2,1)S(1)}, u32[]{:S(2)}, u32[]{:S(2)}) collective-permute-start(bf16[16,1024]{1,0:T(8,128)(2,1)S(1)} %get-tuple-element.38), channel_id=1, source_target_pairs={{0,59},{1,56},{2,57},{3,58},{4,63},{5,60},{6,61},{7,62},{8,0},{9,1... | collective-permute-start | bytes 98312 | tf_op jit(solution)/shard_map/ppermute | solution.py:364
  74.0 1.9 %collective-permute-done.6.xl = bf16[16,1024]{1,0:T(8,128)(2,1)S(1)} collective-permute-done((bf16[16,1024]{1,0:T(8,128)(2,1)S(1)}, bf16[16,1024]{1,0:T(8,128)(2,1)S(1)}, u32[]{:S(2)}, u32[]{:S(2)}) %collective-permute-start.6) | collective-permute-done | bytes 32800 | tf_op jit(solution)/shard_map/ppermute | solution.py:364
  75.9 4.1 %shard_map.63 = bf16[32,72,128]{2,1,0:T(8,128)(2,1)S(1)} custom-call(f32[256,1024]{1,0:T(8,128)S(1)} %get-tuple-element.33.x2, f32[256,1024]{1,0:T(8,128)S(1)} %get-tuple-element.34.d2, bf16[256,1024]{1,0:T(8,128)(2,1)S(1)} %get-tuple-element.26.bt, bf16[256,1024]{1,0:T(8,128)(2,1)S(1)} %get-tuple-element.27.vt, ...), custom_call_target="tpu_custom_call" | custom-call | flops 10000000 | bytes 4000000 | tf_op jit(solution)/shard_map/pallas_call | solution.py:414
  80.0 27.3 %all_to_all.11.recv = bf16[32,72,128]{2,1,0:T(8,128)(2,1)S(1)} all-to-all(bf16[32,72,128]{2,1,0:T(8,128)(2,1)S(1)} %shard_map.63), channel_id=1, replica_groups=mesh['wall'=32,'span'=2,'stream'=4] {'wall'}, dimensions={0} | all-to-all | bytes 1179648 | tf_op jit(solution)/shard_map/all_to_all | solution.py:419
  107.4 1.5 %shard_map.64 = (f32[64,32,128]{2,1,0:T(8,128)S(1)}, f32[4,8,8,128]{3,2,1,0:T(8,128)S(1)}, bf16[4,32,128]{2,1,0:T(8,128)(2,1)S(1)}, bf16[32,128]{1,0:T(8,128)(2,1)S(1)}, bf16[32,128]{1,0:T(8,128)(2,1)S(1)}) custom-call(bf16[32,72,128]{2,1,0:T(8,128)(2,1)S(1)} %all_to_all.11.recv, bf16[2,32,128]{2,1,0:T(8,128)(2,1)S(1)} %get-tuple-element.40.ves, ...), custom_call_target="tpu_custom_call" | custom-call | flops 10000000 | bytes 4000000 | tf_op jit(solution)/shard_map/pallas_call | solution.py:420
  108.9 1.6 %collective-permute-start.8 = (bf16[4,32,128]{2,1,0:T(8,128)(2,1)S(1)}, bf16[4,32,128]{2,1,0:T(8,128)(2,1)S(1)}, u32[]{:S(2)}, u32[]{:S(2)}) collective-permute-start(bf16[4,32,128]{2,1,0:T(8,128)(2,1)S(1)} %get-tuple-element.45), channel_id=1, source_target_pairs={{0,4},{4,0},{1,5},{5,1},{2,6},{6,2},{3,7},{7,3},{8,12},{12,8},{9,1... | collective-permute-start | bytes 98312 | tf_op jit(solution)/shard_map/ppermute | solution.py:346
  110.5 0.5 collective-permute-start.10
  111.0 0.7 collective-permute-done.9.lefts
  111.7 2.2 %collective-permute-done.10.rights = bf16[32,128]{1,0:T(8,128)(2,1)S(1)} collective-permute-done((bf16[32,128]{1,0:T(8,128)(2,1)S(1)}, bf16[32,128]{1,0:T(8,128)(2,1)S(1)}, u32[]{:S(2)}, u32[]{:S(2)}) %collective-permute-start.10) | collective-permute-done | bytes 8224 | tf_op jit(solution)/shard_map/ppermute | solution.py:348
  113.9 5.1 %shard_map.65 = (f32[32,64,128]{2,1,0:T(8,128)}, f32[32,64,128]{2,1,0:T(8,128)}) custom-call(f32[64,32,128]{2,1,0:T(8,128)S(1)} %get-tuple-element.43.xs, f32[2048,128]{1,0:T(8,128)S(1)} %bitcast.4, f32[2048,128]{1,0:T(8,128)S(1)} %bitcast.3, f32[1,32]{1,0:T(1,128)S(1)} %bitcast.6, f32[4,8,8,128]{3,2,1,0:T(8,128)S(1)} %get-tuple-element.44.beyond, ...), custom_call_target="tpu_custom_call" | custom-call | flops 10000000 | bytes 4000000 | tf_op jit(solution)/shard_map/pallas_call | solution.py:434
  (21 shorter events, 0.1 us)
Async XLA Ops:
  0.6 1.2 %copy-start.1 = (f32[32,64,128]{2,1,0:T(8,128)S(1)}, f32[32,64,128]{2,1,0:T(8,128)}, u32[]{:S(2)}) copy-start(f32[32,64,128]{2,1,0:T(8,128)} %b_hbm.1) | copy-start | bytes 3145732
  1.9 1.2 %copy-start.3 = (f32[32,64,128]{2,1,0:T(8,128)S(1)}, f32[32,64,128]{2,1,0:T(8,128)}, u32[]{:S(2)}) copy-start(f32[32,64,128]{2,1,0:T(8,128)} %v_hbm.1) | copy-start | bytes 3145732
  3.1 0.7 copy-start.5
  7.3 51.3 %copy-start = (bf16[1024,1024]{1,0:T(8,128)(2,1)S(1)}, bf16[1024,1024]{1,0:T(8,128)(2,1)}, u32[]{:S(2)}) copy-start(bf16[1024,1024]{1,0:T(8,128)(2,1)} %line.5) | copy-start | bytes 6291460
  50.4 8.9 %collective-permute-start = (bf16[32,1024]{1,0:T(8,128)(2,1)S(1)}, bf16[32,1024]{1,0:T(8,128)(2,1)S(1)}, u32[]{:S(2)}, u32[]{:S(2)}) collective-permute-start(bf16[32,1024]{1,0:T(8,128)(2,1)S(1)} %get-tuple-element.28), channel_id=1, source_target_pairs={{0,64},{1,65},{2,66},{3,67},{4,68},{5,69},{6,70},{7,71},{8,72},{9,... | collective-permute-start | bytes 196616 | tf_op jit(solution)/shard_map/ppermute | solution.py:364
  50.8 8.5 %collective-permute-start.1 = (bf16[32,1024]{1,0:T(8,128)(2,1)S(1)}, bf16[32,1024]{1,0:T(8,128)(2,1)S(1)}, u32[]{:S(2)}, u32[]{:S(2)}) collective-permute-start(bf16[32,1024]{1,0:T(8,128)(2,1)S(1)} %get-tuple-element.29), channel_id=1, source_target_pairs={{0,196},{1,197},{2,198},{3,199},{4,192},{5,193},{6,194},{7,195},{8... | collective-permute-start | bytes 196616 | tf_op jit(solution)/shard_map/ppermute | solution.py:364
  55.6 4.9 %collective-permute-start.2 = (bf16[32,1024]{1,0:T(8,128)(2,1)S(1)}, bf16[32,1024]{1,0:T(8,128)(2,1)S(1)}, u32[]{:S(2)}, u32[]{:S(2)}) collective-permute-start(bf16[32,1024]{1,0:T(8,128)(2,1)S(1)} %get-tuple-element.30), channel_id=1, source_target_pairs={{0,8},{1,9},{2,10},{3,11},{4,12},{5,13},{6,14},{7,15},{8,16},{9,17... | collective-permute-start | bytes 196616 | tf_op jit(solution)/shard_map/ppermute | solution.py:364
  56.1 4.4 %collective-permute-start.3 = (bf16[32,1024]{1,0:T(8,128)(2,1)S(1)}, bf16[32,1024]{1,0:T(8,128)(2,1)S(1)}, u32[]{:S(2)}, u32[]{:S(2)}) collective-permute-start(bf16[32,1024]{1,0:T(8,128)(2,1)S(1)} %get-tuple-element.31), channel_id=1, source_target_pairs={{0,59},{1,56},{2,57},{3,58},{4,63},{5,60},{6,61},{7,62},{8,0},{9,1... | collective-permute-start | bytes 196616 | tf_op jit(solution)/shard_map/ppermute | solution.py:364
  65.3 8.7 %collective-permute-start.4 = (bf16[16,1024]{1,0:T(8,128)(2,1)S(1)}, bf16[16,1024]{1,0:T(8,128)(2,1)S(1)}, u32[]{:S(2)}, u32[]{:S(2)}) collective-permute-start(bf16[16,1024]{1,0:T(8,128)(2,1)S(1)} %get-tuple-element.35), channel_id=1, source_target_pairs={{0,64},{1,65},{2,66},{3,67},{4,68},{5,69},{6,70},{7,71},{8,72},{9,... | collective-permute-start | bytes 98312 | tf_op jit(solution)/shard_map/ppermute | solution.py:364
  65.4 8.6 %collective-permute-start.5 = (bf16[16,1024]{1,0:T(8,128)(2,1)S(1)}, bf16[16,1024]{1,0:T(8,128)(2,1)S(1)}, u32[]{:S(2)}, u32[]{:S(2)}) collective-permute-start(bf16[16,1024]{1,0:T(8,128)(2,1)S(1)} %get-tuple-element.36), channel_id=1, source_target_pairs={{0,196},{1,197},{2,198},{3,199},{4,192},{5,193},{6,194},{7,195},{8... | collective-permute-start | bytes 98312 | tf_op jit(solution)/shard_map/ppermute | solution.py:364
  70.5 5.4 %collective-permute-start.6 = (bf16[16,1024]{1,0:T(8,128)(2,1)S(1)}, bf16[16,1024]{1,0:T(8,128)(2,1)S(1)}, u32[]{:S(2)}, u32[]{:S(2)}) collective-permute-start(bf16[16,1024]{1,0:T(8,128)(2,1)S(1)} %get-tuple-element.37), channel_id=1, source_target_pairs={{0,8},{1,9},{2,10},{3,11},{4,12},{5,13},{6,14},{7,15},{8,16},{9,17... | collective-permute-start | bytes 98312 | tf_op jit(solution)/shard_map/ppermute | solution.py:364
  70.5 5.4 %collective-permute-start.7 = (bf16[16,1024]{1,0:T(8,128)(2,1)S(1)}, bf16[16,1024]{1,0:T(8,128)(2,1)S(1)}, u32[]{:S(2)}, u32[]{:S(2)}) collective-permute-start(bf16[16,1024]{1,0:T(8,128)(2,1)S(1)} %get-tuple-element.38), channel_id=1, source_target_pairs={{0,59},{1,56},{2,57},{3,58},{4,63},{5,60},{6,61},{7,62},{8,0},{9,1... | collective-permute-start | bytes 98312 | tf_op jit(solution)/shard_map/ppermute | solution.py:364
  75.9 38.0 %copy-start.4 = (f32[32,64,128]{2,1,0:T(8,128)S(1)}, f32[32,64,128]{2,1,0:T(8,128)}, u32[]{:S(2)}) copy-start(f32[32,64,128]{2,1,0:T(8,128)} %v_hbm.1) | copy-start | bytes 3145732
  80.0 33.9 %copy-start.2 = (f32[32,64,128]{2,1,0:T(8,128)S(1)}, f32[32,64,128]{2,1,0:T(8,128)}, u32[]{:S(2)}) copy-start(f32[32,64,128]{2,1,0:T(8,128)} %b_hbm.1) | copy-start | bytes 3145732
  80.0 33.9 %copy-start.6 = (f32[32]{0:T(128)S(1)}, f32[32]{0:T(128)}, u32[]{:S(2)}) copy-start(f32[32]{0:T(128)} %param.6) | copy-start | bytes 388
  108.9 5.0 %collective-permute-start.8 = (bf16[4,32,128]{2,1,0:T(8,128)(2,1)S(1)}, bf16[4,32,128]{2,1,0:T(8,128)(2,1)S(1)}, u32[]{:S(2)}, u32[]{:S(2)}) collective-permute-start(bf16[4,32,128]{2,1,0:T(8,128)(2,1)S(1)} %get-tuple-element.45), channel_id=1, source_target_pairs={{0,4},{4,0},{1,5},{5,1},{2,6},{6,2},{3,7},{7,3},{8,12},{12,8},{9,1... | collective-permute-start | bytes 98312 | tf_op jit(solution)/shard_map/ppermute | solution.py:346
  110.5 1.2 collective-permute-start.9
  110.5 3.4 %collective-permute-start.10 = (bf16[32,128]{1,0:T(8,128)(2,1)S(1)}, bf16[32,128]{1,0:T(8,128)(2,1)S(1)}, u32[]{:S(2)}, u32[]{:S(2)}) collective-permute-start(bf16[32,128]{1,0:T(8,128)(2,1)S(1)} %get-tuple-element.47), channel_id=1, source_target_pairs={{1,0},{2,1},{3,2},{0,3},{5,4},{6,5},{7,6},{4,7},{9,8},{10,9},{11,1... | collective-permute-start | bytes 24584 | tf_op jit(solution)/shard_map/ppermute | solution.py:348
